TPU v7x, 128 devices: a whole 4x4x4 slice. The times are simulated.
128 devices in a mesh: row: 8 (over x, y_hi), col: 16 (over y_lo, z, core).
Axes of the slice: x: 4, y: 4 (y_hi: 2, y_lo: 2; y = y_hi * 2 + y_lo), z: 4, core: 2. Of those that a mesh axis runs over, the one named last changes fastest.
Arguments:
- coupling: bfloat16 [32768, 32768], P('row', 'col'), may hold values from -0.03125 to 0.03125
- amplitude: float32 [64, 32768], P(None, 'col'), may hold values from -0.95 to 0.95
- target: float32 [64, 32768], P(None, 'col'), may hold values from -6 to 6
- shadow_target: float32 [64, 32768], P(None, 'col'), may hold values from -10.2 to 10.2
Outputs:
- solution: float32 [64, 32768], P(None, 'col')
- shadow_solution: float32 [64, 32768], P(None, 'col')
- residual: float32 [64, 32768], P(None, 'col')
- shadow_residual: float32 [64, 32768], P(None, 'col')
All inputs are finite; a program needn't handle non-finite values.
Results may differ from a plain program's by a relative error of at most 0.0036.
Values may be sent and summed in bfloat16 or wider, within the bound.
No kernel may reach another device: no remote copies, remote signals or barrier semaphores. Data moves between devices by JAX's collectives and lax.ppermute only.
A program may use at most 128 MiB of HBM per device.

v0:
```python
import jax
import jax.numpy as jnp
from jax import lax
from jax.sharding import PartitionSpec as P

ITERS = 2
SELF_GAIN = 0.5
COUPLE_GAIN = 0.3


def on_device(coupling, amplitude, target, shadow_target):
    row_rows = coupling.shape[0]
    col_rows = coupling.shape[1]
    row_index = lax.axis_index("row")
    col_index = lax.axis_index("col")
    slope = 1.0 - amplitude * amplitude
    solution = jnp.zeros_like(target)
    shadow_solution = jnp.zeros_like(target)
    residual = target
    shadow_residual = shadow_target
    direction = target
    shadow_direction = shadow_target
    align = lax.psum(jnp.sum(shadow_residual * residual, axis=1), "col")
    for iteration in range(ITERS):
        scaled = (slope * direction).astype(jnp.bfloat16)
        primary_gathered = lax.all_gather(scaled, "col", axis=1, tiled=True)
        row_block = lax.dynamic_slice_in_dim(primary_gathered, row_index * row_rows, row_rows, 1)
        primary_partial_value = jnp.dot(row_block, coupling, preferred_element_type=jnp.float32)
        product = lax.psum(primary_partial_value, "row")
        image = direction - SELF_GAIN * slope * direction - COUPLE_GAIN * product
        shadow_scaled = shadow_direction.astype(jnp.bfloat16)
        partial_value = lax.dot_general(
            shadow_scaled, coupling, (((1,), (1,)), ((), ())), preferred_element_type=jnp.float32
        )
        summed = lax.psum(partial_value, "col")
        gathered = lax.all_gather(summed, "row", axis=1, tiled=True)
        own_block = lax.dynamic_slice_in_dim(gathered, col_index * col_rows, col_rows, 1)
        shadow_image = (
            shadow_direction
            - SELF_GAIN * slope * shadow_direction
            - COUPLE_GAIN * slope * own_block
        )
        curve = lax.psum(jnp.sum(shadow_direction * image, axis=1), "col")
        step_size = align / curve
        column_step = step_size[:, None]
        solution = solution + column_step * direction
        shadow_solution = shadow_solution + column_step * shadow_direction
        residual = residual - column_step * image
        shadow_residual = shadow_residual - column_step * shadow_image
        if iteration + 1 < ITERS:
            align_next = lax.psum(jnp.sum(shadow_residual * residual, axis=1), "col")
        if iteration + 1 < ITERS:
            blend = (align_next / align)[:, None]
            direction = residual + blend * direction
            shadow_direction = shadow_residual + blend * shadow_direction
            align = align_next
    return (solution, shadow_solution, residual, shadow_residual)


def solution(mesh):
    return jax.shard_map(
        on_device,
        mesh=mesh,
        in_specs=(P("row", "col"), P(None, "col"), P(None, "col"), P(None, "col")),
        out_specs=(P(None, "col"), P(None, "col"), P(None, "col"), P(None, "col")),
        check_vma=False,
    )
```

profile of v0, /device:TPU:1, one launch (start us, length us, event | category | flops | bytes accessed | tf_op | source)
XLA Modules:
  0.0 766.5 jit_solution(14258358741011477803)
XLA Ops:
  7.2 0.0 all-gather.5.cloned.1.call-start
  7.2 2.1 multiply_convert_fusion.1
  9.3 0.0 all-gather.5.cloned.1.call-update
  9.3 0.0 all-reduce.8.cloned.1.call-start
  9.4 12.1 %fusion.14 = f32[64,4096]{1,0:T(8,128)} fusion(bf16[4096,2048]{1,0:T(8,128)(2,1)} %param.4, f32[64,2048]{1,0:T(8,128)} %param.7), kind=kOutput, calls=%fused_computation.31 | convolution fusion | flops 1073872896 | bytes 18350080 | tf_op jit(solution)/shard_map/dot_general | solution.py:32
  21.5 0.0 copy-start
  21.5 0.0 copy-start.1
  21.5 0.0 copy-start.2
  21.5 0.0 all-reduce.8.cloned.1.call-update
  21.5 0.0 all-reduce.6.cloned.1.call-start
  21.6 29.8 %all-gather.5.cloned.1.call-done = bf16[64,32768]{1,0:T(8,128)(2,1)} async-done(((bf16[64,2048]{1,0:T(8,128)(2,1)}), bf16[64,32768]{1,0:T(8,128)(2,1)}) %all-gather.5.cloned.1.call-update) | async-done | bytes 4194320 | tf_op jit(solution)/shard_map/all_gather | solution.py:26
  51.3 9.8 %fusion.10 = f32[64,2048]{1,0:T(8,128)} fusion(bf16[4096,2048]{1,0:T(8,128)(2,1)} %param.4, bf16[64,32768]{1,0:T(8,128)(2,1)} %all-gather.5.cloned.1.call-done, s32[]{:T(128)S(6)} %select_n.8), kind=kOutput, calls=%fused_computation.24 | convolution fusion | flops 1073741824 | bytes 17825796 | tf_op jit(solution)/shard_map/dot_general | solution.py:28
  61.1 0.0 all-reduce.6.cloned.1.call-update
  61.1 0.0 all-gather.7.cloned.1.call-start
  61.2 111.6 %all-reduce.8.cloned.1.call-done = f32[64,4096]{1,0:T(8,128)} async-done(((f32[64,4096]{1,0:T(8,128)}), f32[64,4096]{1,0:T(8,128)}) %all-reduce.8.cloned.1.call-update) | async-done | bytes 1048592 | tf_op jit(solution)/shard_map/psum | solution.py:35
  172.8 0.0 all-gather.7.cloned.1.call-update
  172.8 0.0 all-gather.9.cloned.1.call-start
  172.9 84.5 %all-reduce.6.cloned.1.call-done = f32[64,2048]{1,0:T(8,128)} async-done(((f32[64,2048]{1,0:T(8,128)}), f32[64,2048]{1,0:T(8,128)}) %all-reduce.6.cloned.1.call-update) | async-done | bytes 524304 | tf_op jit(solution)/shard_map/psum | solution.py:29
  257.3 0.0 copy-done
  257.3 0.0 copy-done.1
  257.3 0.0 copy-done.2
  257.3 1.3 multiply_reduce_fusion.2
  258.7 32.6 %all-reduce = (f32[64]{0:T(128)S(1)}, f32[64]{0:T(128)S(1)}) all-reduce(f32[64]{0:T(128)S(1)} %get-tuple-element.5, f32[64]{0:T(128)S(1)} %get-tuple-element.4), channel_id=1, replica_groups=mesh['row'=8,'col'=16] {'col'}, use_global_device_ids=true, to_apply=%region_1.0 | all-reduce | flops 128 | bytes 1024 | tf_op jit(solution)/shard_map/psum | solution.py:23
  291.3 79.8 %all-gather.7.cloned.1.call-done = f32[64,32768]{1,0:T(8,128)} async-done(((f32[64,4096]{1,0:T(8,128)}), f32[64,32768]{1,0:T(8,128)}) %all-gather.7.cloned.1.call-update) | async-done | bytes 8388624 | tf_op jit(solution)/shard_map/all_gather | solution.py:36
  371.0 1.6 multiply_reduce_fusion.1
  372.7 27.6 %psum.60 = f32[64]{0:T(128)S(1)} all-reduce(f32[64]{0:T(128)S(1)} %get-tuple-element.10), channel_id=1, replica_groups=mesh['row'=8,'col'=16] {'col'}, use_global_device_ids=true, to_apply=%region_7.0 | all-reduce | flops 64 | bytes 512 | tf_op jit(solution)/shard_map/psum | solution.py:51
  400.3 0.9 multiply_convert_fusion
  401.1 0.0 all-gather.9.cloned.1.call-update
  401.1 0.0 all-reduce.12.cloned.1.call-start
  401.2 12.0 %fusion.12 = f32[64,4096]{1,0:T(8,128)} fusion(bf16[4096,2048]{1,0:T(8,128)(2,1)} %param.4, f32[64,2048]{1,0:T(8,128)S(1)} %get-tuple-element.12, f32[64,2048]{1,0:T(8,128)S(1)} %copy-done, f32[64]{0:T(128)S(1)} %div.10), kind=kOutput, calls=%fused_computation.29 | convolution fusion | flops 1074135040 | bytes 18874624 | tf_op jit(solution)/shard_map/dot_general | solution.py:32
  413.2 0.0 all-reduce.12.cloned.1.call-update
  413.2 0.2 all-reduce.10.cloned.1.call-start
  413.4 23.9 %all-gather.9.cloned.1.call-done = bf16[64,32768]{1,0:T(8,128)(2,1)} async-done(((bf16[64,2048]{1,0:T(8,128)(2,1)}), bf16[64,32768]{1,0:T(8,128)(2,1)}) %all-gather.9.cloned.1.call-update) | async-done | bytes 4194320 | tf_op jit(solution)/shard_map/all_gather | solution.py:26
  437.4 9.8 %fusion.8 = f32[64,2048]{1,0:T(8,128)} fusion(bf16[4096,2048]{1,0:T(8,128)(2,1)} %param.4, bf16[64,32768]{1,0:T(8,128)(2,1)} %all-gather.9.cloned.1.call-done, s32[]{:T(128)S(6)} %select_n.8), kind=kOutput, calls=%fused_computation.16 | convolution fusion | flops 1073741824 | bytes 17825796 | tf_op jit(solution)/shard_map/dot_general | solution.py:28
  447.1 0.0 all-reduce.10.cloned.1.call-update
  447.1 0.0 all-gather.11.cloned.1.call-start
  447.2 111.4 %all-reduce.12.cloned.1.call-done = f32[64,4096]{1,0:T(8,128)} async-done(((f32[64,4096]{1,0:T(8,128)}), f32[64,4096]{1,0:T(8,128)}) %all-reduce.12.cloned.1.call-update) | async-done | bytes 1048592 | tf_op jit(solution)/shard_map/psum | solution.py:35
  558.6 0.0 all-gather.11.cloned.1.call-update
  558.7 84.5 %all-reduce.10.cloned.1.call-done = f32[64,2048]{1,0:T(8,128)} async-done(((f32[64,2048]{1,0:T(8,128)}), f32[64,2048]{1,0:T(8,128)}) %all-reduce.10.cloned.1.call-update) | async-done | bytes 524304 | tf_op jit(solution)/shard_map/psum | solution.py:29
  643.2 1.4 multiply_reduce_fusion
  644.6 32.6 %psum.62 = f32[64]{0:T(128)S(1)} all-reduce(f32[64]{0:T(128)S(1)} %get-tuple-element.8), channel_id=1, replica_groups=mesh['row'=8,'col'=16] {'col'}, use_global_device_ids=true, to_apply=%region_10.0 | all-reduce | flops 64 | bytes 512 | tf_op jit(solution)/shard_map/psum | solution.py:43
  677.2 79.8 %all-gather.11.cloned.1.call-done = f32[64,32768]{1,0:T(8,128)} async-done(((f32[64,4096]{1,0:T(8,128)}), f32[64,32768]{1,0:T(8,128)}) %all-gather.11.cloned.1.call-update) | async-done | bytes 8388624 | tf_op jit(solution)/shard_map/all_gather | solution.py:36
  757.0 2.7 multiply_subtract_fusion.4
  (3 shorter events, 0.0 us)
Async XLA Ops:
  7.2 44.2 %all-gather.5.cloned.1.call-start = ((), (), s32[]{:S(2)}) async-start(), calls=%async_computation | async-start | bytes 4456448 | tf_op jit(solution)/shard_map/all_gather | solution.py:26
  9.3 163.5 %all-reduce.8.cloned.1.call-start = ((), (), s32[]{:S(2)}) async-start(), calls=%async_computation.2 | async-start | bytes 2097152 | tf_op jit(solution)/shard_map/psum | solution.py:35
  21.5 235.8 %copy-start = (f32[64,2048]{1,0:T(8,128)S(1)}, f32[64,2048]{1,0:T(8,128)}, u32[]{:S(2)}) copy-start(f32[64,2048]{1,0:T(8,128)} %param.7) | copy-start | bytes 1572868
  21.5 235.8 %copy-start.1 = (f32[64,2048]{1,0:T(8,128)S(1)}, f32[64,2048]{1,0:T(8,128)}, u32[]{:S(2)}) copy-start(f32[64,2048]{1,0:T(8,128)} %param.6) | copy-start | bytes 1572868
  21.5 235.8 %copy-start.2 = (f32[64,2048]{1,0:T(8,128)S(1)}, f32[64,2048]{1,0:T(8,128)}, u32[]{:S(2)}) copy-start(f32[64,2048]{1,0:T(8,128)} %param.5) | copy-start | bytes 1572868
  21.5 235.8 %all-reduce.6.cloned.1.call-start = ((), (), s32[]{:S(2)}) async-start(), calls=%async_computation.1 | async-start | bytes 1048576 | tf_op jit(solution)/shard_map/psum | solution.py:29
  61.1 309.9 %all-gather.7.cloned.1.call-start = ((), (), s32[]{:S(2)}) async-start(), calls=%async_computation.3 | async-start | bytes 9437184 | tf_op jit(solution)/shard_map/all_gather | solution.py:36
  172.8 264.5 %all-gather.9.cloned.1.call-start = ((), (), s32[]{:S(2)}) async-start(), calls=%async_computation.4 | async-start | bytes 4456448 | tf_op jit(solution)/shard_map/all_gather | solution.py:26
  401.1 157.5 %all-reduce.12.cloned.1.call-start = ((), (), s32[]{:S(2)}) async-start(), calls=%async_computation.6 | async-start | bytes 2097152 | tf_op jit(solution)/shard_map/psum | solution.py:35
  413.2 230.0 %all-reduce.10.cloned.1.call-start = ((), (), s32[]{:S(2)}) async-start(), calls=%async_computation.5 | async-start | bytes 1048576 | tf_op jit(solution)/shard_map/psum | solution.py:29
  447.1 309.9 %all-gather.11.cloned.1.call-start = ((), (), s32[]{:S(2)}) async-start(), calls=%async_computation.7 | async-start | bytes 9437184 | tf_op jit(solution)/shard_map/all_gather | solution.py:36
Sparse Core Ops, SparseCore 0:
  10.2 41.0 all-gather.4
  53.8 118.9 all-reduce.7
  176.0 81.2 all-reduce.5
  259.5 111.4 all-gather.6
  401.2 36.0 all-gather.8
  439.7 118.9 all-reduce.11
  561.9 81.2 all-reduce.9
  645.5 111.4 all-gather.10
where the time goes:
time: 767 us
  waiting for transfers between devices  605 us (79%)
  blocking collectives  92.8 us (12%)
  matrix products  43.6 us (6%)
  between operations  14.2 us (2%)
  other arithmetic  10 us (1%)
    psum x2, waiting for transfers between devices, on_device(): summed = lax.psum(partial_value, 'col')  223 us
    psum x2, waiting for transfers between devices, on_device(): product = lax.psum(primary_partial_value, 'row')  169 us
    all_gather x2, waiting for transfers between devices, on_device(): gathered = lax.all_gather(summed, 'row', axis=1, tiled=True)  160 us
    all_gather x2, waiting for transfers between devices, on_device(): primary_gathered = lax.all_gather(scaled, 'col', axis=1, tiled=True)  53.7 us
    psum x1, blocking collectives, on_device(): curve = lax.psum(jnp.sum(shadow_direction * image, axis=1), 'col')  32.6 us
    psum x1, blocking collectives, on_device(): align = lax.psum(jnp.sum(shadow_residual * residual, axis=1), 'col')  32.6 us
    psum x1, blocking collectives, on_device(): align_next = lax.psum(jnp.sum(shadow_residual * residual, axis=1), 'col')  27.6 us
    dot_general x2, matrix products, on_device(): lax.dot_general(shadow_scaled, coupling, (((1,), (1,)), ((), ())), prefer...  24.1 us
  transfers between devices with their start and end apart: 8, of which 8 were waited for; matrix products, arithmetic and copies ran while one was open for 6% of the time, Pallas kernels for 0%

commit v1 on v0

--- a/solution.py
+++ b/solution.py
@@ -33,7 +33,10 @@
             shadow_scaled, coupling, (((1,), (1,)), ((), ())), preferred_element_type=jnp.float32
         )
         summed = lax.psum(partial_value, "col")
-        gathered = lax.all_gather(summed, "row", axis=1, tiled=True)
+        count = lax.axis_size("row")
+        blocks = jnp.stack([summed for _ in range(count)])
+        blocks = lax.all_to_all(blocks, "row", split_axis=0, concat_axis=0)
+        gathered = jnp.concatenate(blocks, axis=1)
         own_block = lax.dynamic_slice_in_dim(gathered, col_index * col_rows, col_rows, 1)
         shadow_image = (
             shadow_direction

time: 767 us -> 801 us (1.044)
  local copies, waits for them, and re-layouts: 0.01 us -> 26.3 us
  starting transfers between devices: 0.51 us -> 12.7 us
    all_gather x2, waiting for transfers between devices: 53.7 us -> 222 us  [on_device(): primary_gathered = lax.all_gather(scaled, 'col', axis=1, tiled=True)]
    all_gather x2 -> x0, waiting for transfers between devices: 160 us -> none  [on_device(): gathered = lax.all_gather(summed, 'row', axis=1, tiled=True)]
    psum x2, waiting for transfers between devices: 169 us -> 144 us  [on_device(): product = lax.psum(primary_partial_value, 'row')]
    reshape x0 -> x2, local copies, waits for them, and re-layouts: none -> 15.2 us  [on_device(): gathered = jnp.concatenate(blocks, axis=1)]
    psum x2, waiting for transfers between devices: 223 us -> 236 us  [on_device(): summed = lax.psum(partial_value, 'col')]
    all_to_all x0 -> x2, starting transfers between devices: none -> 12.3 us  [on_device(): blocks = lax.all_to_all(blocks, 'row', split_axis=0, concat_axis=0)]
    another operation x0 -> x2, local copies, waits for them, and re-layouts: none -> 11 us  [on_device(): blocks = jnp.stack([summed for _ in range(count)])]
  transfers between devices with their start and end apart: 8 -> 8, of which waited for: 8 -> 6; matrix products, arithmetic and copies ran while one was open for 6% -> 6% of each run, Pallas kernels for 0% -> 0%
where the time goes in v1:
time: 801 us; the launch traced here: 800 us
  waiting for transfers between devices  603 us (75%)
  blocking collectives  91.9 us (11%)
  matrix products  43.8 us (5%)
  local copies, waits for them, and re-layouts  26.3 us (3%)
  between operations  14.2 us (2%)
  starting transfers between devices  12.7 us (2%)
  other arithmetic  8.68 us (1%)
    psum x2, waiting for transfers between devices, on_device(): summed = lax.psum(partial_value, 'col')  236 us
    all_gather x2, waiting for transfers between devices, on_device(): primary_gathered = lax.all_gather(scaled, 'col', axis=1, tiled=True)  222 us
    psum x2, waiting for transfers between devices, on_device(): product = lax.psum(primary_partial_value, 'row')  144 us
    psum x1, blocking collectives, on_device(): align = lax.psum(jnp.sum(shadow_residual * residual, axis=1), 'col')  32.4 us
    psum x1, blocking collectives, on_device(): curve = lax.psum(jnp.sum(shadow_direction * image, axis=1), 'col')  32.4 us
    psum x1, blocking collectives, on_device(): align_next = lax.psum(jnp.sum(shadow_residual * residual, axis=1), 'col')  27.1 us
    dot_general x2, matrix products, on_device(): lax.dot_general(shadow_scaled, coupling, (((1,), (1,)), ((), ())), prefer...  24.3 us
    dot_general x2, matrix products, on_device(): jnp.dot(row_block, coupling, preferred_element_type=jnp.float32)  19.5 us
  transfers between devices with their start and end apart: 8, of which 6 were waited for; matrix products, arithmetic and copies ran while one was open for 6% of the time, Pallas kernels for 0%

profile of v1, /device:TPU:1, one launch (start us, length us, event | category | flops | bytes accessed | tf_op | source)
XLA Modules:
  0.0 800.1 jit_solution(9298472651001695556)
XLA Ops:
  7.2 0.0 copy-start.2
  7.2 0.0 copy-start.1
  7.2 0.0 all-reduce.8.cloned.1.call-start
  7.2 12.2 %fusion.14 = f32[64,4096]{1,0:T(8,128)} fusion(bf16[4096,2048]{1,0:T(8,128)(2,1)} %param.4, f32[64,2048]{1,0:T(8,128)} %param.7), kind=kOutput, calls=%fused_computation.31 | convolution fusion | flops 1073872896 | bytes 18350080 | tf_op jit(solution)/shard_map/dot_general | solution.py:32
  19.5 0.0 all-reduce.8.cloned.1.call-update
  19.5 0.0 all-gather.3.cloned.1.call-start
  19.5 0.0 copy-done.2
  19.5 0.0 copy-done.1
  19.6 0.8 multiply_convert_fusion.1
  20.3 0.0 all-gather.3.cloned.1.call-update
  20.3 122.1 %all-reduce.8.cloned.1.call-done = f32[64,4096]{1,0:T(8,128)} async-done(((f32[64,4096]{1,0:T(8,128)}), f32[64,4096]{1,0:T(8,128)}) %all-reduce.8.cloned.1.call-update) | async-done | bytes 1048592 | tf_op jit(solution)/shard_map/psum | solution.py:35
  142.4 5.5 stack.4
  148.0 6.1 all-to-all-start
  154.1 0.0 all-reduce.6.cloned.1.call-start
  154.1 111.1 %all-gather.3.cloned.1.call-done = bf16[64,32768]{1,0:T(8,128)(2,1)} async-done(((bf16[64,2048]{1,0:T(8,128)(2,1)}), bf16[64,32768]{1,0:T(8,128)(2,1)}) %all-gather.3.cloned.1.call-update) | async-done | bytes 4194320 | tf_op jit(solution)/shard_map/all_gather | solution.py:26
  265.2 9.8 %fusion.10 = f32[64,2048]{1,0:T(8,128)} fusion(bf16[4096,2048]{1,0:T(8,128)(2,1)} %param.4, bf16[64,32768]{1,0:T(8,128)(2,1)} %all-gather.3.cloned.1.call-done, s32[]{:T(128)S(6)} %select_n.8), kind=kOutput, calls=%fused_computation.24 | convolution fusion | flops 1073741824 | bytes 17825796 | tf_op jit(solution)/shard_map/dot_general | solution.py:28
  275.0 0.0 all-reduce.6.cloned.1.call-update
  275.0 0.0 all-reduce.12.cloned.1.call-start
  275.1 0.0 all-to-all-done
  275.1 0.0 copy-start
  275.1 7.6 copy.10
  282.8 72.1 %all-reduce.6.cloned.1.call-done = f32[64,2048]{1,0:T(8,128)} async-done(((f32[64,2048]{1,0:T(8,128)}), f32[64,2048]{1,0:T(8,128)}) %all-reduce.6.cloned.1.call-update) | async-done | bytes 524304 | tf_op jit(solution)/shard_map/psum | solution.py:29
  354.8 0.0 copy-done
  354.8 1.3 multiply_reduce_fusion.2
  356.2 32.4 %all-reduce = (f32[64]{0:T(128)S(1)}, f32[64]{0:T(128)S(1)}) all-reduce(f32[64]{0:T(128)S(1)} %get-tuple-element.5, f32[64]{0:T(128)S(1)} %get-tuple-element.4), channel_id=1, replica_groups=mesh['row'=8,'col'=16] {'col'}, use_global_device_ids=true, to_apply=%region_1.0 | all-reduce | flops 128 | bytes 1024 | tf_op jit(solution)/shard_map/psum | solution.py:23
  388.6 1.6 multiply_reduce_fusion.1
  390.2 27.1 %psum.60 = f32[64]{0:T(128)S(1)} all-reduce(f32[64]{0:T(128)S(1)} %get-tuple-element.10), channel_id=1, replica_groups=mesh['row'=8,'col'=16] {'col'}, use_global_device_ids=true, to_apply=%region_7.0 | all-reduce | flops 64 | bytes 512 | tf_op jit(solution)/shard_map/psum | solution.py:54
  417.3 12.0 %fusion.12 = f32[64,4096]{1,0:T(8,128)} fusion(bf16[4096,2048]{1,0:T(8,128)(2,1)} %param.4, f32[64,2048]{1,0:T(8,128)S(1)} %get-tuple-element.12, f32[64,2048]{1,0:T(8,128)S(1)} %copy-done, f32[64]{0:T(128)S(1)} %div.10), kind=kOutput, calls=%fused_computation.29 | convolution fusion | flops 1074135040 | bytes 18874624 | tf_op jit(solution)/shard_map/dot_general | solution.py:32
  429.4 0.0 all-reduce.12.cloned.1.call-update
  429.4 0.2 all-gather.5.cloned.1.call-start
  429.6 0.8 multiply_convert_fusion
  430.5 0.0 all-gather.5.cloned.1.call-update
  430.5 113.9 %all-reduce.12.cloned.1.call-done = f32[64,4096]{1,0:T(8,128)} async-done(((f32[64,4096]{1,0:T(8,128)}), f32[64,4096]{1,0:T(8,128)}) %all-reduce.12.cloned.1.call-update) | async-done | bytes 1048592 | tf_op jit(solution)/shard_map/psum | solution.py:35
  544.4 5.5 stack.5
  549.9 6.1 all-to-all-start.1
  556.0 0.0 all-reduce.10.cloned.1.call-start
  556.1 111.1 %all-gather.5.cloned.1.call-done = bf16[64,32768]{1,0:T(8,128)(2,1)} async-done(((bf16[64,2048]{1,0:T(8,128)(2,1)}), bf16[64,32768]{1,0:T(8,128)(2,1)}) %all-gather.5.cloned.1.call-update) | async-done | bytes 4194320 | tf_op jit(solution)/shard_map/all_gather | solution.py:26
  667.2 9.8 %fusion.8 = f32[64,2048]{1,0:T(8,128)} fusion(bf16[4096,2048]{1,0:T(8,128)(2,1)} %param.4, bf16[64,32768]{1,0:T(8,128)(2,1)} %all-gather.5.cloned.1.call-done, s32[]{:T(128)S(6)} %select_n.8), kind=kOutput, calls=%fused_computation.16 | convolution fusion | flops 1073741824 | bytes 17825796 | tf_op jit(solution)/shard_map/dot_general | solution.py:28
  677.0 0.0 all-reduce.10.cloned.1.call-update
  677.0 0.0 all-to-all-done.1
  677.0 7.6 copy.11
  684.6 72.2 %all-reduce.10.cloned.1.call-done = f32[64,2048]{1,0:T(8,128)} async-done(((f32[64,2048]{1,0:T(8,128)}), f32[64,2048]{1,0:T(8,128)}) %all-reduce.10.cloned.1.call-update) | async-done | bytes 524304 | tf_op jit(solution)/shard_map/psum | solution.py:29
  756.8 1.4 multiply_reduce_fusion
  758.2 32.4 %psum.62 = f32[64]{0:T(128)S(1)} all-reduce(f32[64]{0:T(128)S(1)} %get-tuple-element.8), channel_id=1, replica_groups=mesh['row'=8,'col'=16] {'col'}, use_global_device_ids=true, to_apply=%region_10.0 | all-reduce | flops 64 | bytes 512 | tf_op jit(solution)/shard_map/psum | solution.py:46
  790.6 2.7 multiply_subtract_fusion.4
  (3 shorter events, 0.0 us)
Async XLA Ops:
  7.2 12.4 %copy-start.2 = (f32[64,2048]{1,0:T(8,128)S(1)}, f32[64,2048]{1,0:T(8,128)}, u32[]{:S(2)}) copy-start(f32[64,2048]{1,0:T(8,128)} %param.5) | copy-start | bytes 1572868
  7.2 12.4 %copy-start.1 = (f32[64,2048]{1,0:T(8,128)S(1)}, f32[64,2048]{1,0:T(8,128)}, u32[]{:S(2)}) copy-start(f32[64,2048]{1,0:T(8,128)} %param.6) | copy-start | bytes 1572868
  7.2 135.3 %all-reduce.8.cloned.1.call-start = ((), (), s32[]{:S(2)}) async-start(), calls=%async_computation.4 | async-start | bytes 2097152 | tf_op jit(solution)/shard_map/psum | solution.py:35
  19.5 245.8 %all-gather.3.cloned.1.call-start = ((), (), s32[]{:S(2)}) async-start(), calls=%async_computation.2 | async-start | bytes 4456448 | tf_op jit(solution)/shard_map/all_gather | solution.py:26
  148.0 127.1 %all-to-all-start = ((f32[8,64,4096]{2,1,0:T(8,128)}), f32[8,64,4096]{2,1,0:T(8,128)}, u32[]{:S(2)}, u32[]{:S(2)}) async-start(f32[8,64,4096]{2,1,0:T(8,128)} %stack.4), calls=%async_computation | async-start | bytes 16777216 | tf_op jit(solution)/shard_map/all_to_all | solution.py:38
  154.1 200.7 %all-reduce.6.cloned.1.call-start = ((), (), s32[]{:S(2)}) async-start(), calls=%async_computation.3 | async-start | bytes 1048576 | tf_op jit(solution)/shard_map/psum | solution.py:29
  275.0 269.3 %all-reduce.12.cloned.1.call-start = ((), (), s32[]{:S(2)}) async-start(), calls=%async_computation.7 | async-start | bytes 2097152 | tf_op jit(solution)/shard_map/psum | solution.py:35
  275.1 79.7 %copy-start = (f32[64,2048]{1,0:T(8,128)S(1)}, f32[64,2048]{1,0:T(8,128)}, u32[]{:S(2)}) copy-start(f32[64,2048]{1,0:T(8,128)} %param.7) | copy-start | bytes 1572868
  429.4 237.8 %all-gather.5.cloned.1.call-start = ((), (), s32[]{:S(2)}) async-start(), calls=%async_computation.5 | async-start | bytes 4456448 | tf_op jit(solution)/shard_map/all_gather | solution.py:26
  549.9 127.1 %all-to-all-start.1 = ((f32[8,64,4096]{2,1,0:T(8,128)}), f32[8,64,4096]{2,1,0:T(8,128)}, u32[]{:S(2)}, u32[]{:S(2)}) async-start(f32[8,64,4096]{2,1,0:T(8,128)} %stack.5), calls=%async_computation.1 | async-start | bytes 16777216 | tf_op jit(solution)/shard_map/all_to_all | solution.py:38
  556.0 200.7 %all-reduce.10.cloned.1.call-start = ((), (), s32[]{:S(2)}) async-start(), calls=%async_computation.6 | async-start | bytes 1048576 | tf_op jit(solution)/shard_map/psum | solution.py:29
Sparse Core Ops, SparseCore 0:
  19.6 122.7 all-reduce.7
  144.8 120.4 all-gather.2
  275.2 79.6 all-reduce.5
  429.5 114.8 all-reduce.11
  546.6 120.5 all-gather.4
  677.1 79.6 all-reduce.9
